TPU v7x, 32 devices: a whole 2x2x4 slice. The times are simulated.
32 devices in a mesh: band: 8 (over z, y), feat: 4 (over x, core).
Axes of the slice: x: 2, y: 2, z: 4, core: 2. Of those that a mesh axis runs over, the one named last changes fastest.
Arguments:
- grid_latent: bfloat16 [2048, 512], P('band', 'feat'), may hold values from -6 to 6
- mesh_latent: bfloat16 [2048, 512], P('band', 'feat'), may hold values from -6 to 6
- w_grid: bfloat16 [512, 512], P(None, 'feat'), may hold values from -0.25 to 0.25
- w_mesh: bfloat16 [512, 512], P(None, 'feat'), may hold values from -0.25 to 0.25
- w_enc_out: bfloat16 [512, 512], P('feat'), may hold values from -0.25 to 0.25
- w_send: bfloat16 [512, 512], P(None, 'feat'), may hold values from -0.25 to 0.25
- w_recv: bfloat16 [512, 512], P(None, 'feat'), may hold values from -0.25 to 0.25
- w_proc_out: bfloat16 [512, 512], P('feat'), may hold values from -0.25 to 0.25
- grid_send: int32 [64, 64], P('band'), may hold values from 0 to 255
- g2m_src: int32 [64, 128], P('band'), may hold values from 0 to 511
- g2m_dst: int32 [64, 128], P('band'), may hold values from 0 to 255
- mesh_send: int32 [64, 32], P('band'), may hold values from 0 to 255
- m2m_src: int32 [64, 128], P('band'), may hold values from 0 to 511
- m2m_dst: int32 [64, 128], P('band'), may hold values from 0 to 255
- cotangent: bfloat16 [2048, 512], P('band', 'feat'), may hold values from -6 to 6
Outputs:
- mesh_out: bfloat16 [2048, 512], P('band', 'feat')
- grid_grad: bfloat16 [2048, 512], P('band', 'feat')
- grad_w_grid: float32 [512, 512], P(None, 'feat')
- grad_w_mesh: float32 [512, 512], P(None, 'feat')
- grad_w_enc_out: float32 [512, 512], P('feat')
- grad_w_send: float32 [512, 512], P(None, 'feat')
- grad_w_recv: float32 [512, 512], P(None, 'feat')
- grad_w_proc_out: float32 [512, 512], P('feat')
Inputs may be any that keep to these rules, and one draw needn't show every extreme that they name: `grid_send`: local grid row indices of the sending band. `mesh_send`: local mesh row indices of the sending partition. `m2m_src`: values under 256 are own rows, the rest halo slots.
All inputs are finite; a program needn't handle non-finite values.
Results may differ from a plain program's by a relative error of at most 0.014.
Values may be sent and summed in bfloat16 or wider, within the bound.
A program may use at most 64 MiB of HBM per device.

v0:
```python
import math

import jax
import jax.numpy as jnp
from jax import lax
from jax.sharding import PartitionSpec as P


def silu_slope(values):
    sigma = jax.nn.sigmoid(values)
    return sigma * (1.0 + values * (1.0 - sigma))


def matmul(left, right):
    return jnp.dot(left, right, preferred_element_type=jnp.float32)


def inner_rows(left, right):
    return lax.dot_general(
        left, right, (((0,), (0,)), ((), ())), preferred_element_type=jnp.float32
    )


def hot_table(index, count):
    return (index[:, None] == lax.iota(jnp.int32, count)[None, :]).astype(jnp.bfloat16)


def per_device(
    grid_latent,
    mesh_latent,
    w_grid,
    w_mesh,
    w_enc_out,
    w_send,
    w_recv,
    w_proc_out,
    grid_send,
    g2m_src,
    g2m_dst,
    mesh_send,
    m2m_src,
    m2m_dst,
    cotangent,
):
    bands = lax.axis_size("band")
    grid_rows = grid_latent.shape[0]
    mesh_rows = mesh_latent.shape[0]
    hidden_dev = w_grid.shape[1]
    halo_rows = bands * mesh_send.shape[1]
    slot_rows = bands * grid_send.shape[1]
    scale = 1.0 / math.sqrt(mesh_rows * bands)
    enc_source = g2m_src.reshape(-1)
    enc_target = g2m_dst.reshape(-1)
    proc_source = m2m_src.reshape(-1)
    proc_target = m2m_dst.reshape(-1)
    enc_columns, proc_columns = (
        lax.all_to_all(w_enc_out, "feat", split_axis=1, concat_axis=0, tiled=True),
        lax.all_to_all(w_proc_out, "feat", split_axis=1, concat_axis=0, tiled=True),
    )
    send_slice, recv_slice, grid_slice = (
        lax.all_to_all(w_send, "feat", split_axis=0, concat_axis=1, tiled=True),
        lax.all_to_all(w_recv, "feat", split_axis=0, concat_axis=1, tiled=True),
        lax.all_to_all(w_grid, "feat", split_axis=0, concat_axis=1, tiled=True),
    )
    grid_full = lax.all_gather(grid_latent, "feat", axis=1, tiled=True)
    mesh_full = lax.all_gather(mesh_latent, "feat", axis=1, tiled=True)
    proj_grid = matmul(grid_full, w_grid).astype(jnp.bfloat16)
    outgoing = jnp.take(proj_grid, grid_send, axis=0)
    arrived = lax.all_to_all(outgoing, "band", split_axis=0, concat_axis=0, tiled=True)
    slot_proj = arrived.reshape(slot_rows, hidden_dev)
    proj_mesh = matmul(mesh_full, w_mesh).astype(jnp.bfloat16)
    enc_pre = jnp.take(slot_proj, enc_source, axis=0).astype(jnp.float32) + jnp.take(
        proj_mesh, enc_target, axis=0
    ).astype(jnp.float32)
    enc_active = jax.nn.silu(enc_pre).astype(jnp.bfloat16)
    enc_table = hot_table(enc_target, mesh_rows)
    enc_summed = inner_rows(enc_table, enc_active).astype(jnp.bfloat16)
    enc_whole = lax.all_gather(enc_summed, "feat", axis=1, tiled=True)
    update = matmul(enc_whole, enc_columns)
    mesh_mid = (mesh_latent.astype(jnp.float32) + update).astype(jnp.bfloat16)
    mid_full = lax.all_gather(mesh_mid, "feat", axis=1, tiled=True)
    proj_send = matmul(mid_full, w_send).astype(jnp.bfloat16)
    proj_recv = matmul(mid_full, w_recv).astype(jnp.bfloat16)
    halo_out = jnp.take(proj_send, mesh_send, axis=0)
    halo_in = lax.all_to_all(halo_out, "band", split_axis=0, concat_axis=0, tiled=True)
    extended = jnp.concatenate([proj_send, halo_in.reshape(halo_rows, hidden_dev)], axis=0)
    proc_pre = jnp.take(extended, proc_source, axis=0).astype(jnp.float32) + jnp.take(
        proj_recv, proc_target, axis=0
    ).astype(jnp.float32)
    proc_active = jax.nn.silu(proc_pre).astype(jnp.bfloat16)
    proc_table = hot_table(proc_target, mesh_rows)
    proc_summed = inner_rows(proc_table, proc_active).astype(jnp.bfloat16)
    proc_whole = lax.all_gather(proc_summed, "feat", axis=1, tiled=True)
    proc_update = matmul(proc_whole, proc_columns)
    mesh_out = (mesh_mid.astype(jnp.float32) + proc_update).astype(jnp.bfloat16)
    cot_full = lax.all_gather(cotangent, "feat", axis=1, tiled=True)
    back_proc = matmul(cot_full, w_proc_out.T).astype(jnp.bfloat16)
    grad_proc_out = inner_rows(proc_summed, cot_full)
    slope_proc = (
        jnp.take(back_proc, proc_target, axis=0).astype(jnp.float32) * silu_slope(proc_pre)
    ).astype(jnp.bfloat16)
    back_recv = inner_rows(proc_table, slope_proc).astype(jnp.bfloat16)
    source_table = hot_table(proc_source, mesh_rows + halo_rows)
    back_ext = inner_rows(source_table, slope_proc).astype(jnp.bfloat16)
    back_halo = back_ext[mesh_rows:].reshape(bands, halo_rows // bands, hidden_dev)
    returned = lax.all_to_all(back_halo, "band", split_axis=0, concat_axis=0, tiled=True)
    returned_sum = jax.ops.segment_sum(
        returned.reshape(halo_rows, hidden_dev).astype(jnp.float32),
        mesh_send.reshape(-1),
        num_segments=mesh_rows,
    )
    back_send = (back_ext[:mesh_rows].astype(jnp.float32) + returned_sum).astype(jnp.bfloat16)
    grad_send = inner_rows(mid_full, back_send)
    grad_recv = inner_rows(mid_full, back_recv)
    send_whole, recv_whole = (
        lax.all_gather(back_send, "feat", axis=1, tiled=True),
        lax.all_gather(back_recv, "feat", axis=1, tiled=True),
    )
    back_sum = matmul(send_whole, send_slice.T) + matmul(recv_whole, recv_slice.T)
    back_mid = (cotangent.astype(jnp.float32) + back_sum).astype(jnp.bfloat16)
    back_full = lax.all_gather(back_mid, "feat", axis=1, tiled=True)
    back_enc = matmul(back_full, w_enc_out.T).astype(jnp.bfloat16)
    grad_enc_out = inner_rows(enc_summed, back_full)
    slope_enc = (
        jnp.take(back_enc, enc_target, axis=0).astype(jnp.float32) * silu_slope(enc_pre)
    ).astype(jnp.bfloat16)
    back_pmesh = inner_rows(enc_table, slope_enc).astype(jnp.bfloat16)
    grad_mesh_w = inner_rows(mesh_full, back_pmesh)
    slot_table = hot_table(enc_source, slot_rows)
    back_slot = inner_rows(slot_table, slope_enc).astype(jnp.bfloat16)
    back_slots = lax.all_to_all(
        back_slot.reshape(bands, slot_rows // bands, hidden_dev),
        "band",
        split_axis=0,
        concat_axis=0,
        tiled=True,
    )
    back_pgrid = jax.ops.segment_sum(
        back_slots.reshape(slot_rows, hidden_dev).astype(jnp.float32),
        grid_send.reshape(-1),
        num_segments=grid_rows,
    ).astype(jnp.bfloat16)
    grad_grid_w = inner_rows(grid_full, back_pgrid)
    pgrid_whole = lax.all_gather(back_pgrid, "feat", axis=1, tiled=True)
    grid_grad = matmul(pgrid_whole, grid_slice.T).astype(jnp.bfloat16)
    grad_grid_w, grad_mesh_w, grad_enc_out, grad_send, grad_recv, grad_proc_out = lax.psum(
        (grad_grid_w, grad_mesh_w, grad_enc_out, grad_send, grad_recv, grad_proc_out), "band"
    )
    return (
        mesh_out,
        grid_grad,
        grad_grid_w * scale,
        grad_mesh_w * scale,
        grad_enc_out * scale,
        grad_send * scale,
        grad_recv * scale,
        grad_proc_out * scale,
    )


def solution(mesh):
    in_specs = (
        P("band", "feat"),
        P("band", "feat"),
        P(None, "feat"),
        P(None, "feat"),
        P("feat", None),
        P(None, "feat"),
        P(None, "feat"),
        P("feat", None),
        P("band", None),
        P("band", None),
        P("band", None),
        P("band", None),
        P("band", None),
        P("band", None),
        P("band", "feat"),
    )
    out_specs = (
        P("band", "feat"),
        P("band", "feat"),
        P(None, "feat"),
        P(None, "feat"),
        P("feat", None),
        P(None, "feat"),
        P(None, "feat"),
        P("feat", None),
    )
    return jax.shard_map(
        per_device, mesh=mesh, in_specs=in_specs, out_specs=out_specs, check_vma=False
    )
```

profile of v0, /device:TPU:0, one launch (start us, length us, event | category | flops | bytes accessed | tf_op | source)
XLA Modules:
  0.0 257.3 jit_solution(16485318864674626195)
XLA Ops:
  9.0 4.3 %all-to-all-start.1 = ((bf16[128,4,128]{0,2,1:T(8,128)(2,1)}), bf16[128,4,128]{0,2,1:T(8,128)(2,1)S(1)}, u32[]{:S(2)}, u32[]{:S(2)}) async-start(bf16[128,4,128]{0,2,1:T(8,128)(2,1)} %bitcast.4), calls=%async_computation.1 | async-start | bytes 262144 | tf_op jit(solution)/shard_map/all_to_all | solution.py:57
  13.4 6.8 %all_gather.31 = bf16[256,512]{1,0:T(8,128)(2,1)S(1)} all-gather(bf16[256,128]{1,0:T(8,128)(2,1)S(1)} %copy-done.9), channel_id=1, replica_groups=mesh['band'=8,'feat'=4] {'feat'}, dimensions={1}, use_global_device_ids=true | all-gather | bytes 327680 | tf_op jit(solution)/shard_map/all_gather | solution.py:66
  20.2 5.9 %all_gather.30 = bf16[256,512]{1,0:T(8,128)(2,1)S(1)} all-gather(bf16[256,128]{1,0:T(8,128)(2,1)S(1)} %copy-done.10), channel_id=1, replica_groups=mesh['band'=8,'feat'=4] {'feat'}, dimensions={1}, use_global_device_ids=true | all-gather | bytes 327680 | tf_op jit(solution)/shard_map/all_gather | solution.py:65
  26.2 5.9 %all_gather.35 = bf16[256,512]{1,0:T(8,128)(2,1)S(1)} all-gather(bf16[256,128]{1,0:T(8,128)(2,1)S(1)} %copy-done.3), channel_id=1, replica_groups=mesh['band'=8,'feat'=4] {'feat'}, dimensions={1}, use_global_device_ids=true | all-gather | bytes 327680 | tf_op jit(solution)/shard_map/all_gather | solution.py:96
  36.4 3.3 %all-to-all-start.5 = ((bf16[4,128,128]{2,1,0:T(8,128)(2,1)}), bf16[4,128,128]{2,1,0:T(8,128)(2,1)S(1)}, u32[]{:S(2)}, u32[]{:S(2)}) async-start(bf16[4,128,128]{2,1,0:T(8,128)(2,1)} %bitcast.16), calls=%async_computation.5 | async-start | bytes 262144 | tf_op jit(solution)/shard_map/all_to_all | solution.py:61
  39.8 4.6 %all-to-all-done.5 = bf16[4,128,128]{2,1,0:T(8,128)(2,1)S(1)} async-done(((bf16[4,128,128]{2,1,0:T(8,128)(2,1)}), bf16[4,128,128]{2,1,0:T(8,128)(2,1)S(1)}, u32[]{:S(2)}, u32[]{:S(2)}) %all-to-all-start.5) | async-done | bytes 131104 | tf_op jit(solution)/shard_map/all_to_all | solution.py:61
  44.3 3.3 %all-to-all-start.6 = ((bf16[4,128,128]{2,1,0:T(8,128)(2,1)}), bf16[4,128,128]{2,1,0:T(8,128)(2,1)S(1)}, u32[]{:S(2)}, u32[]{:S(2)}) async-start(bf16[4,128,128]{2,1,0:T(8,128)(2,1)} %bitcast.19), calls=%async_computation.6 | async-start | bytes 262144 | tf_op jit(solution)/shard_map/all_to_all | solution.py:62
  47.8 4.5 %all-to-all-done.6 = bf16[4,128,128]{2,1,0:T(8,128)(2,1)S(1)} async-done(((bf16[4,128,128]{2,1,0:T(8,128)(2,1)}), bf16[4,128,128]{2,1,0:T(8,128)(2,1)S(1)}, u32[]{:S(2)}, u32[]{:S(2)}) %all-to-all-start.6) | async-done | bytes 131104 | tf_op jit(solution)/shard_map/all_to_all | solution.py:62
  52.3 6.4 %all-to-all-start = ((bf16[8,64,128]{2,1,0:T(8,128)(2,1)}), bf16[8,64,128]{2,1,0:T(8,128)(2,1)S(1)}, u32[]{:S(2)}, u32[]{:S(2)}) async-start(bf16[8,64,128]{2,1,0:T(8,128)(2,1)} %broadcast_select_fusion.4), calls=%async_computation | async-start | bytes 262144 | tf_op jit(solution)/shard_map/all_to_all | solution.py:69
  58.8 3.2 %gather_fusion.3 = bf16[1024,128]{1,0:T(8,128)(2,1)S(1)} fusion(bf16[256,128]{1,0:T(8,128)(2,1)S(1)} %convolution_convert_fusion.9, s32[1024]{0:T(1024)S(1)} %fusion.21), kind=kCustom, calls=%fused_computation.1.clone | custom fusion | bytes 528384 | tf_op jit(solution)/shard_map/jit(_take)/gather | solution.py:72
  62.0 3.2 %gather_fusion.6 = bf16[1024,128]{1,0:T(8,128)(2,1)S(1)} fusion(bf16[256,128]{1,0:T(8,128)(2,1)S(1)} %convolution_convert_fusion.4, s32[1024]{0:T(1024)S(1)} %fusion.23), kind=kCustom, calls=%fused_computation.4.clone | custom fusion | bytes 528384 | tf_op jit(solution)/shard_map/jit(_take)/gather | solution.py:100
  66.0 3.2 %gather_fusion.2 = bf16[1024,128]{1,0:T(8,128)(2,1)S(1)} fusion(bf16[512,128]{1,0:T(8,128)(2,1)S(1)} %bitcast.78, s32[1024]{0:T(1024)S(1)} %fusion.20), kind=kCustom, calls=%fused_computation.clone | custom fusion | bytes 528384 | tf_op jit(solution)/shard_map/jit(_take)/gather | solution.py:72
  70.1 5.8 %all_gather.32 = bf16[256,512]{1,0:T(8,128)(2,1)S(1)} all-gather(bf16[256,128]{1,0:T(8,128)(2,1)S(1)} %convolution_convert_fusion.8), channel_id=1, replica_groups=mesh['band'=8,'feat'=4] {'feat'}, dimensions={1}, use_global_device_ids=true | all-gather | bytes 327680 | tf_op jit(solution)/shard_map/all_gather | solution.py:78
  76.1 5.9 %all_gather.33 = bf16[256,512]{1,0:T(8,128)(2,1)S(1)} all-gather(bf16[256,128]{1,0:T(8,128)(2,1)S(1)} %fusion.5), channel_id=1, replica_groups=mesh['band'=8,'feat'=4] {'feat'}, dimensions={1}, use_global_device_ids=true | all-gather | bytes 327680 | tf_op jit(solution)/shard_map/all_gather | solution.py:81
  84.7 5.7 %all-to-all-start.2 = ((bf16[8,32,128]{2,1,0:T(8,128)(2,1)}), bf16[8,32,128]{2,1,0:T(8,128)(2,1)S(1)}, u32[]{:S(2)}, u32[]{:S(2)}) async-start(bf16[8,32,128]{2,1,0:T(8,128)(2,1)} %broadcast_select_fusion.9), calls=%async_computation.2 | async-start | bytes 131072 | tf_op jit(solution)/shard_map/all_to_all | solution.py:85
  91.5 3.2 %gather_fusion.5 = bf16[1024,128]{1,0:T(8,128)(2,1)S(1)} fusion(bf16[256,128]{1,0:T(8,128)(2,1)S(1)} %convolution_convert_fusion.6, s32[1024]{0:T(1024)S(1)} %fusion.23), kind=kCustom, calls=%fused_computation.3.clone | custom fusion | bytes 528384 | tf_op jit(solution)/shard_map/jit(_take)/gather | solution.py:87
  94.8 2.6 all-to-all-done.2
  97.3 3.2 %gather_fusion.4 = bf16[1024,128]{1,0:T(8,128)(2,1)S(1)} fusion(bf16[512,128]{1,0:T(8,128)(2,1)S(1)} %pad_maximum_fusion, s32[1024]{0:T(1024)S(1)} %fusion.22), kind=kCustom, calls=%fused_computation.2.clone | custom fusion | bytes 528384 | tf_op jit(solution)/shard_map/jit(_take)/gather | solution.py:87
  104.4 3.4 %all-to-all-start.4 = ((bf16[8,32,128]{2,1,0:T(8,128)(2,1)}), bf16[8,32,128]{2,1,0:T(8,128)(2,1)S(1)}, u32[]{:S(2)}, u32[]{:S(2)}) async-start(bf16[8,32,128]{2,1,0:T(8,128)(2,1)} %bitcast.14), calls=%async_computation.4 | async-start | bytes 131072 | tf_op jit(solution)/shard_map/all_to_all | solution.py:106
  109.7 5.8 %all_gather.37 = bf16[256,512]{1,0:T(8,128)(2,1)S(1)} all-gather(bf16[256,128]{1,0:T(8,128)(2,1)S(1)} %convolution_convert_fusion.3), channel_id=1, replica_groups=mesh['band'=8,'feat'=4] {'feat'}, dimensions={1}, use_global_device_ids=true | all-gather | bytes 327680 | tf_op jit(solution)/shard_map/all_gather | solution.py:117
  117.5 5.9 %all_gather.36 = bf16[256,512]{1,0:T(8,128)(2,1)S(1)} all-gather(bf16[256,128]{1,0:T(8,128)(2,1)S(1)} %convert_element_type.136), channel_id=1, replica_groups=mesh['band'=8,'feat'=4] {'feat'}, dimensions={1}, use_global_device_ids=true | all-gather | bytes 327680 | tf_op jit(solution)/shard_map/all_gather | solution.py:116
  123.9 6.2 %all_gather.38 = bf16[256,512]{1,0:T(8,128)(2,1)S(1)} all-gather(bf16[256,128]{1,0:T(8,128)(2,1)S(1)} %fusion.7), channel_id=1, replica_groups=mesh['band'=8,'feat'=4] {'feat'}, dimensions={1}, use_global_device_ids=true | all-gather | bytes 327680 | tf_op jit(solution)/shard_map/all_gather | solution.py:121
  131.2 3.2 %gather_fusion.7 = bf16[1024,128]{1,0:T(8,128)(2,1)S(1)} fusion(bf16[256,128]{1,0:T(8,128)(2,1)S(1)} %convolution_convert_fusion.2, s32[1024]{0:T(1024)S(1)} %fusion.21), kind=kCustom, calls=%fused_computation.5.clone | custom fusion | bytes 528384 | tf_op jit(solution)/shard_map/jit(_take)/gather | solution.py:125
  138.3 6.0 %all-to-all-start.7 = ((bf16[8,64,128]{2,1,0:T(8,128)(2,1)}), bf16[8,64,128]{2,1,0:T(8,128)(2,1)S(1)}, u32[]{:S(2)}, u32[]{:S(2)}) async-start(bf16[8,64,128]{2,1,0:T(8,128)(2,1)} %bitcast.22), calls=%async_computation.7 | async-start | bytes 262144 | tf_op jit(solution)/shard_map/all_to_all | solution.py:131
  145.3 6.5 %all-to-all-done.7 = bf16[8,64,128]{2,1,0:T(8,128)(2,1)S(1)} async-done(((bf16[8,64,128]{2,1,0:T(8,128)(2,1)}), bf16[8,64,128]{2,1,0:T(8,128)(2,1)S(1)}, u32[]{:S(2)}, u32[]{:S(2)}) %all-to-all-start.7) | async-done | bytes 131104 | tf_op jit(solution)/shard_map/all_to_all | solution.py:131
  151.8 2.3 scatter_custom_fusion.1
  155.2 7.0 %all_to_all.115 = bf16[128,4,128]{0,2,1:T(8,128)(2,1)S(1)} all-to-all(bf16[128,4,128]{0,2,1:T(8,128)(2,1)S(1)} %bitcast.88), channel_id=1, replica_groups=mesh['band'=8,'feat'=4] {'feat'}, dimensions={1} | all-to-all | bytes 262144 | tf_op jit(solution)/shard_map/all_to_all | solution.py:58
  162.2 3.3 %all-to-all-start.8 = ((bf16[4,128,128]{2,1,0:T(8,128)(2,1)}), bf16[4,128,128]{2,1,0:T(8,128)(2,1)S(1)}, u32[]{:S(2)}, u32[]{:S(2)}) async-start(bf16[4,128,128]{2,1,0:T(8,128)(2,1)} %bitcast.24), calls=%async_computation.8 | async-start | bytes 262144 | tf_op jit(solution)/shard_map/all_to_all | solution.py:63
  165.7 4.5 %all-to-all-done.8 = bf16[4,128,128]{2,1,0:T(8,128)(2,1)S(1)} async-done(((bf16[4,128,128]{2,1,0:T(8,128)(2,1)}), bf16[4,128,128]{2,1,0:T(8,128)(2,1)S(1)}, u32[]{:S(2)}, u32[]{:S(2)}) %all-to-all-start.8) | async-done | bytes 131104 | tf_op jit(solution)/shard_map/all_to_all | solution.py:63
  170.3 5.8 %all_gather.34 = bf16[256,512]{1,0:T(8,128)(2,1)S(1)} all-gather(bf16[256,128]{1,0:T(8,128)(2,1)S(1)} %convolution_convert_fusion.5), channel_id=1, replica_groups=mesh['band'=8,'feat'=4] {'feat'}, dimensions={1}, use_global_device_ids=true | all-gather | bytes 327680 | tf_op jit(solution)/shard_map/all_gather | solution.py:93
  177.0 5.9 %all_gather.39 = bf16[256,512]{1,0:T(8,128)(2,1)S(1)} all-gather(bf16[256,128]{1,0:T(8,128)(2,1)S(1)} %convert_element_type.145), channel_id=1, replica_groups=mesh['band'=8,'feat'=4] {'feat'}, dimensions={1}, use_global_device_ids=true | all-gather | bytes 327680 | tf_op jit(solution)/shard_map/all_gather | solution.py:144
  183.7 60.1 %all-reduce.3.cloned.1.call-done = (f32[512,128]{0,1:T(8,128)}, f32[512,128]{0,1:T(8,128)}, f32[128,512]{1,0:T(8,128)}, f32[512,128]{0,1:T(8,128)}, f32[512,128]{0,1:T(8,128)}, /*index=5*/f32[128,512]{1,0:T(8,128)}) async-done(((f32[512,128]{0,1:T(8,128)}, f32[512,128]{0,1:T(8,128)}, f32[128,512]{1,0:T(8,128)}, f32[512,128]{0,1:T(8,128)}, f32[512,128]{0,1:T(8,128)}, /*index=5*/f32[128,512]{1,0:T(8,128)}), ...) | async-done | bytes 1572880 | tf_op jit(solution)/shard_map/psum | solution.py:146
  (105 shorter events, 35.7 us)
Async XLA Ops:
  7.2 25.0 %copy-start = (bf16[512,128]{1,0:T(8,128)(2,1)S(1)}, bf16[512,128]{1,0:T(8,128)(2,1)}, u32[]{:S(2)}) copy-start(bf16[512,128]{1,0:T(8,128)(2,1)} %param.22) | copy-start | bytes 393220
  7.2 6.1 %copy-start.12 = (s32[8,64]{1,0:T(8,128)S(1)}, s32[8,64]{1,0:T(8,128)}, u32[]{:S(2)}) copy-start(s32[8,64]{1,0:T(8,128)} %param.27) | copy-start | bytes 6148
  7.2 6.1 %copy-start.11 = (s32[8,128]{1,0:T(8,128)S(1)}, s32[8,128]{1,0:T(8,128)}, u32[]{:S(2)}) copy-start(s32[8,128]{1,0:T(8,128)} %param.29) | copy-start | bytes 12292
  7.2 6.1 %copy-start.16 = (s32[8,128]{1,0:T(8,128)S(1)}, s32[8,128]{1,0:T(8,128)}, u32[]{:S(2)}) copy-start(s32[8,128]{1,0:T(8,128)} %param.28) | copy-start | bytes 12292
  7.2 6.2 %copy-start.9 = (bf16[256,128]{1,0:T(8,128)(2,1)S(1)}, bf16[256,128]{1,0:T(8,128)(2,1)}, u32[]{:S(2)}) copy-start(bf16[256,128]{1,0:T(8,128)(2,1)} %param.20) | copy-start | bytes 196612
  9.0 11.2 %copy-start.10 = (bf16[256,128]{1,0:T(8,128)(2,1)S(1)}, bf16[256,128]{1,0:T(8,128)(2,1)}, u32[]{:S(2)}) copy-start(bf16[256,128]{1,0:T(8,128)(2,1)} %param.19) | copy-start | bytes 196612
  9.0 27.4 %all-to-all-start.1 = ((bf16[128,4,128]{0,2,1:T(8,128)(2,1)}), bf16[128,4,128]{0,2,1:T(8,128)(2,1)S(1)}, u32[]{:S(2)}, u32[]{:S(2)}) async-start(bf16[128,4,128]{0,2,1:T(8,128)(2,1)} %bitcast.4), calls=%async_computation.1 | async-start | bytes 262144 | tf_op jit(solution)/shard_map/all_to_all | solution.py:57
  13.4 12.8 %copy-start.14 = (s32[8,128]{1,0:T(8,128)S(1)}, s32[8,128]{1,0:T(8,128)}, u32[]{:S(2)}) copy-start(s32[8,128]{1,0:T(8,128)} %param.32) | copy-start | bytes 12292
  13.4 12.8 %copy-start.3 = (bf16[256,128]{1,0:T(8,128)(2,1)S(1)}, bf16[256,128]{1,0:T(8,128)(2,1)}, u32[]{:S(2)}) copy-start(bf16[256,128]{1,0:T(8,128)(2,1)} %param.33) | copy-start | bytes 196612
  34.8 0.9 copy-start.2
  35.7 0.7 copy-start.13
  35.7 4.0 %copy-start.15 = (s32[8,128]{1,0:T(8,128)S(1)}, s32[8,128]{1,0:T(8,128)}, u32[]{:S(2)}) copy-start(s32[8,128]{1,0:T(8,128)} %param.31) | copy-start | bytes 12292
  36.4 7.9 %all-to-all-start.5 = ((bf16[4,128,128]{2,1,0:T(8,128)(2,1)}), bf16[4,128,128]{2,1,0:T(8,128)(2,1)S(1)}, u32[]{:S(2)}, u32[]{:S(2)}) async-start(bf16[4,128,128]{2,1,0:T(8,128)(2,1)} %bitcast.16), calls=%async_computation.5 | async-start | bytes 262144 | tf_op jit(solution)/shard_map/all_to_all | solution.py:61
  44.3 7.9 %all-to-all-start.6 = ((bf16[4,128,128]{2,1,0:T(8,128)(2,1)}), bf16[4,128,128]{2,1,0:T(8,128)(2,1)S(1)}, u32[]{:S(2)}, u32[]{:S(2)}) async-start(bf16[4,128,128]{2,1,0:T(8,128)(2,1)} %bitcast.19), calls=%async_computation.6 | async-start | bytes 262144 | tf_op jit(solution)/shard_map/all_to_all | solution.py:62
  52.3 13.7 %all-to-all-start = ((bf16[8,64,128]{2,1,0:T(8,128)(2,1)}), bf16[8,64,128]{2,1,0:T(8,128)(2,1)S(1)}, u32[]{:S(2)}, u32[]{:S(2)}) async-start(bf16[8,64,128]{2,1,0:T(8,128)(2,1)} %broadcast_select_fusion.4), calls=%async_computation | async-start | bytes 262144 | tf_op jit(solution)/shard_map/all_to_all | solution.py:69
  84.7 12.6 %all-to-all-start.2 = ((bf16[8,32,128]{2,1,0:T(8,128)(2,1)}), bf16[8,32,128]{2,1,0:T(8,128)(2,1)S(1)}, u32[]{:S(2)}, u32[]{:S(2)}) async-start(bf16[8,32,128]{2,1,0:T(8,128)(2,1)} %broadcast_select_fusion.9), calls=%async_computation.2 | async-start | bytes 131072 | tf_op jit(solution)/shard_map/all_to_all | solution.py:85
  104.4 11.1 %all-to-all-start.4 = ((bf16[8,32,128]{2,1,0:T(8,128)(2,1)}), bf16[8,32,128]{2,1,0:T(8,128)(2,1)S(1)}, u32[]{:S(2)}, u32[]{:S(2)}) async-start(bf16[8,32,128]{2,1,0:T(8,128)(2,1)} %bitcast.14), calls=%async_computation.4 | async-start | bytes 131072 | tf_op jit(solution)/shard_map/all_to_all | solution.py:106
  123.8 6.2 %copy-start.1 = (bf16[128,512]{1,0:T(8,128)(2,1)S(1)}, bf16[128,512]{1,0:T(8,128)(2,1)}, u32[]{:S(2)}) copy-start(bf16[128,512]{1,0:T(8,128)(2,1)} %param.23) | copy-start | bytes 393220
  138.3 13.5 %all-to-all-start.7 = ((bf16[8,64,128]{2,1,0:T(8,128)(2,1)}), bf16[8,64,128]{2,1,0:T(8,128)(2,1)S(1)}, u32[]{:S(2)}, u32[]{:S(2)}) async-start(bf16[8,64,128]{2,1,0:T(8,128)(2,1)} %bitcast.22), calls=%async_computation.7 | async-start | bytes 262144 | tf_op jit(solution)/shard_map/all_to_all | solution.py:131
  144.3 99.5 %all-reduce.3.cloned.1.call-start = ((), (), s32[]{:S(2)}) async-start(), calls=%async_computation.9 | async-start | bytes 3145728 | tf_op jit(solution)/shard_map/psum | solution.py:146
  162.2 7.9 %all-to-all-start.8 = ((bf16[4,128,128]{2,1,0:T(8,128)(2,1)}), bf16[4,128,128]{2,1,0:T(8,128)(2,1)S(1)}, u32[]{:S(2)}, u32[]{:S(2)}) async-start(bf16[4,128,128]{2,1,0:T(8,128)(2,1)} %bitcast.24), calls=%async_computation.8 | async-start | bytes 262144 | tf_op jit(solution)/shard_map/all_to_all | solution.py:63
  244.8 1.0 copy-start.8
  245.8 1.0 copy-start.7
  246.7 1.0 copy-start.6
  247.8 1.0 copy-start.5
  248.8 1.0 copy-start.4
Sparse Core Ops, SparseCore 0:
  155.2 88.5 all-reduce.2
where the time goes:
time: 259 us; the launch traced here: 257 us
  waiting for transfers between devices  83.1 us (32%)
  blocking collectives  67 us (26%)
  starting transfers between devices  35.9 us (14%)
  local copies, waits for them, and re-layouts  28.9 us (11%)
  matrix products  17.3 us (7%)
  between operations  14.5 us (6%)
  other arithmetic  10.6 us (4%)
    psum x1, waiting for transfers between devices, per_device(): lax.psum((grad_grid_w, grad_mesh_w, grad_enc_out, grad_send, grad_recv, g...  60.1 us
    dot_general x11, matrix products, inner_rows(): lax.dot_general(left, right, (((0,), (0,)), ((), ())), preferred_element_...  11 us
    all_to_all x1, blocking collectives, per_device(): lax.all_to_all(w_proc_out, 'feat', split_axis=1, concat_axis=0, tiled=True)  7.02 us
    all_gather x1, blocking collectives, per_device(): mesh_full = lax.all_gather(mesh_latent, 'feat', axis=1, tiled=True)  6.78 us
    unnamed x40, local copies, waits for them, and re-layouts  6.55 us
    all_to_all x1, waiting for transfers between devices, per_device(): lax.all_to_all(back_slot.reshape(bands, slot_rows // bands, hidden_dev),...  6.51 us
    all_to_all x1, starting transfers between devices, per_device(): lax.all_to_all(outgoing, 'band', split_axis=0, concat_axis=0, tiled=True)  6.36 us
    dot_general x11, matrix products, matmul(): return jnp.dot(left, right, preferred_element_type=jnp.float32)  6.31 us
  transfers between devices with their start and end apart: 9, of which 7 were waited for; matrix products, arithmetic and copies ran while one was open for 8% of the time, Pallas kernels for 0%

commit v1 on v0

--- a/solution.py
+++ b/solution.py
@@ -1,8 +1,11 @@
+import functools
 import math
 
 import jax
 import jax.numpy as jnp
 from jax import lax
+from jax.experimental import pallas as pl
+from jax.experimental.pallas import tpu as pltpu
 from jax.sharding import PartitionSpec as P
 
 
@@ -25,7 +28,7 @@
     return (index[:, None] == lax.iota(jnp.int32, count)[None, :]).astype(jnp.bfloat16)
 
 
-def per_device(
+def per_device_collectives(
     grid_latent,
     mesh_latent,
     w_grid,
@@ -158,6 +161,515 @@
     )
 
 
+def inner_columns(left, right):
+    return lax.dot_general(
+        left, right, (((1,), (1,)), ((), ())), preferred_element_type=jnp.float32
+    )
+
+
+def hot(condition):
+    return jnp.where(condition, 1.0, 0.0).astype(jnp.bfloat16)
+
+
+def sigmoid(values):
+    return 1.0 / (1.0 + jnp.exp(-values))
+
+
+def fused_kernel(
+    bands,
+    feats,
+    scale,
+    grid_latent,
+    mesh_latent,
+    w_grid,
+    w_mesh,
+    w_enc_out,
+    w_send,
+    w_recv,
+    w_proc_out,
+    grid_send,
+    g2m_src,
+    g2m_dst,
+    mesh_send,
+    m2m_src,
+    m2m_dst,
+    cotangent,
+    mesh_out,
+    grid_grad,
+    out_grid,
+    out_mesh,
+    out_enc,
+    out_send,
+    out_recv,
+    out_proc,
+    index_rows,
+    index_columns,
+    grid_full,
+    mesh_full,
+    cot_full,
+    enc_full,
+    send_full,
+    recv_full,
+    proc_columns,
+    grid_slice,
+    grid_pick,
+    mesh_pick,
+    enc_gather,
+    enc_scatter,
+    proc_gather,
+    proc_scatter,
+    enc_rows,
+    proc_rows,
+    outgoing,
+    halo_out,
+    enc_pre,
+    back_edge,
+    edge_values,
+    edge_slopes,
+    enc_whole,
+    mid_full,
+    proc_whole,
+    recv_whole,
+    send_whole,
+    back_full,
+    back_ext,
+    halo_back,
+    back_slot,
+    slot_back,
+    pgrid_whole,
+    tall_part,
+    tall_land,
+    tall_sum,
+    wide_part,
+    wide_land,
+    wide_sum,
+    feat_send_sem,
+    feat_recv_sem,
+    band_send_sem,
+    band_recv_sem,
+):
+    band = lax.axis_index("band")
+    feat = lax.axis_index("feat")
+    width = grid_latent.shape[1]
+    rows = mesh_latent.shape[0]
+    grid_rows = grid_latent.shape[0]
+    slot_peer = grid_send.shape[1]
+    halo_peer = mesh_send.shape[1]
+    slots = bands * slot_peer
+    halos = bands * halo_peer
+    edge_rows = g2m_src.shape[0]
+    lanes = g2m_src.shape[1]
+    ext = rows + halos
+    started = []
+
+    def column(place):
+        return pl.ds(pl.multiple_of(place * width, width), width)
+
+    def block(place, size):
+        return pl.ds(pl.multiple_of(place * size, size), size)
+
+    barrier = pltpu.get_barrier_semaphore()
+    for step in range(1, bands):
+        pl.semaphore_signal(
+            barrier,
+            inc=1,
+            device_id={"band": lax.rem(band + step, bands)},
+            device_id_type=pl.DeviceIdType.MESH,
+        )
+    for step in range(1, feats):
+        pl.semaphore_signal(
+            barrier,
+            inc=1,
+            device_id={"feat": lax.rem(feat + step, feats)},
+            device_id_type=pl.DeviceIdType.MESH,
+        )
+    pl.semaphore_wait(barrier, bands + feats - 2)
+
+    counts = {"feat": 0, "band": 0}
+
+    def exchange(axis, source, target):
+        me, size, send_sem, recv_sem = (
+            (feat, feats, feat_send_sem, feat_recv_sem)
+            if axis == "feat"
+            else (band, bands, band_send_sem, band_recv_sem)
+        )
+        phase = counts[axis]
+        counts[axis] += 1
+        copies = []
+        for step in range(1, size):
+            peer = lax.rem(me + step, size)
+            copy = pltpu.make_async_remote_copy(
+                src_ref=source(peer),
+                dst_ref=target(me),
+                send_sem=send_sem.at[phase, step - 1],
+                recv_sem=recv_sem.at[phase, step - 1],
+                device_id={axis: peer},
+                device_id_type=pl.DeviceIdType.MESH,
+            )
+            copy.start()
+            copies.append(copy)
+        started.extend(copies)
+        return copies
+
+    def arrive(copies):
+        for copy in copies:
+            copy.wait_recv()
+
+    def gather_columns(source, target):
+        copies = exchange("feat", lambda peer: source, lambda me: target.at[:, column(me)])
+        target[:, column(feat)] = source[...]
+        return copies
+
+    def gather_held(target):
+        mine = target.at[:, column(feat)]
+        return exchange("feat", lambda peer: mine, lambda me: mine)
+
+    grid_copies = gather_columns(grid_latent, grid_full)
+    mesh_copies = gather_columns(mesh_latent, mesh_full)
+
+    index_rows[...] = jnp.zeros_like(index_rows)
+    index_rows[0:edge_rows, :] = g2m_src[...]
+    index_rows[edge_rows : 2 * edge_rows, :] = g2m_dst[...]
+    index_rows[2 * edge_rows : 3 * edge_rows, :] = m2m_src[...]
+    index_rows[3 * edge_rows : 4 * edge_rows, :] = m2m_dst[...]
+    index_rows[4 * edge_rows : 4 * edge_rows + bands, 0:slot_peer] = grid_send[...]
+    index_rows[4 * edge_rows + bands : 4 * edge_rows + 2 * bands, 0:halo_peer] = mesh_send[...]
+    index_columns[...] = index_rows[...].T
+
+    def picks(target, first, size, count):
+        place = lax.broadcasted_iota(jnp.int32, (size, count), 1)
+        for peer in range(bands):
+            chosen = index_columns[0:size, first + peer : first + peer + 1]
+            target[peer * size : (peer + 1) * size, :] = hot(chosen == place)
+
+    def edge_gather(target, first, start, count):
+        place = lax.broadcasted_iota(jnp.int32, (lanes, count), 1)
+        for row in range(edge_rows):
+            chosen = index_columns[:, first + row : first + row + 1]
+            target[row * lanes : (row + 1) * lanes, start : start + count] = hot(chosen == place)
+
+    def edge_scatter(target, index, start, count):
+        place = lax.broadcasted_iota(jnp.int32, (count, lanes), 0)
+        for row in range(edge_rows):
+            chosen = index[row : row + 1, :]
+            target[start : start + count, row * lanes : (row + 1) * lanes] = hot(chosen == place)
+
+    picks(grid_pick, 4 * edge_rows, slot_peer, grid_rows)
+
+    arrive(grid_copies)
+    proj_grid = matmul(grid_full[...], w_grid[...]).astype(jnp.bfloat16)
+    outgoing[...] = matmul(grid_pick[...], proj_grid).astype(jnp.bfloat16)
+    slot_copies = exchange(
+        "band",
+        lambda peer: outgoing.at[block(peer, slot_peer)],
+        lambda me: enc_rows.at[block(me, slot_peer)],
+    )
+    enc_rows[block(band, slot_peer), :] = outgoing[block(band, slot_peer), :]
+    arrive(mesh_copies)
+    enc_full[block(feat, width), :] = w_enc_out[...]
+    enc_weight_copies = exchange(
+        "feat", lambda peer: w_enc_out, lambda me: enc_full.at[block(me, width)]
+    )
+    cot_copies = gather_columns(cotangent, cot_full)
+    enc_rows[slots : slots + rows, :] = matmul(mesh_full[...], w_mesh[...]).astype(jnp.bfloat16)
+    edge_gather(enc_gather, 0, 0, slots)
+    edge_gather(enc_gather, edge_rows, slots, rows)
+    edge_scatter(enc_scatter, g2m_dst, slots, rows)
+
+    def per_chunk(body):
+        size = 2 * lanes
+
+        def step(place, carry):
+            body(pl.ds(pl.multiple_of(place * size, size), size))
+            return carry
+
+        lax.fori_loop(0, edge_rows // 2, step, 0)
+
+    arrive(slot_copies)
+
+    def enc_forward(edges):
+        values = matmul(enc_gather[edges, :], enc_rows[...])
+        enc_pre[edges, :] = values
+        edge_values[edges, :] = (values * sigmoid(values)).astype(jnp.bfloat16)
+
+    per_chunk(enc_forward)
+    enc_summed = matmul(enc_scatter[slots : slots + rows, :], edge_values[...])
+    enc_whole[:, column(feat)] = enc_summed.astype(jnp.bfloat16)
+    enc_copies = gather_held(enc_whole)
+
+    def enc_slope(edges):
+        enc_pre[edges, :] = silu_slope_of(enc_pre[edges, :])
+
+    per_chunk(enc_slope)
+    picks(mesh_pick, 4 * edge_rows + bands, halo_peer, rows)
+    edge_gather(proc_gather, 2 * edge_rows, 0, ext)
+    edge_gather(proc_gather, 3 * edge_rows, ext, rows)
+    arrive(enc_weight_copies)
+    arrive(enc_copies)
+    mid_full[...] = (
+        mesh_full[...].astype(jnp.float32) + matmul(enc_whole[...], enc_full[...])
+    ).astype(jnp.bfloat16)
+    proj_send = matmul(mid_full[...], w_send[...]).astype(jnp.bfloat16)
+    halo_out[...] = matmul(mesh_pick[...], proj_send).astype(jnp.bfloat16)
+    halo_copies = exchange(
+        "band",
+        lambda peer: halo_out.at[block(peer, halo_peer)],
+        lambda me: proc_rows.at[pl.ds(pl.multiple_of(rows + me * halo_peer, halo_peer), halo_peer)],
+    )
+    send_weight_copies = gather_columns(w_send, send_full)
+    recv_weight_copies = gather_columns(w_recv, recv_full)
+    proc_rows[pl.ds(pl.multiple_of(rows + band * halo_peer, halo_peer), halo_peer), :] = halo_out[
+        block(band, halo_peer), :
+    ]
+    proc_rows[0:rows, :] = proj_send
+    proc_rows[ext : ext + rows, :] = matmul(mid_full[...], w_recv[...]).astype(jnp.bfloat16)
+    arrive(cot_copies)
+    back_proc = inner_columns(cot_full[...], w_proc_out[...]).astype(jnp.bfloat16)
+    back_edge[...] = matmul(proc_gather[:, ext : ext + rows], back_proc)
+    edge_scatter(proc_scatter, m2m_src, 0, ext)
+    edge_scatter(proc_scatter, m2m_dst, ext, rows)
+    arrive(halo_copies)
+
+    def proc_forward(edges):
+        values = matmul(proc_gather[edges, :], proc_rows[...])
+        sigma = sigmoid(values)
+        edge_values[edges, :] = (values * sigma).astype(jnp.bfloat16)
+        slope = sigma * (1.0 + values * (1.0 - sigma))
+        edge_slopes[edges, :] = (back_edge[edges, :] * slope).astype(jnp.bfloat16)
+
+    per_chunk(proc_forward)
+    back_ext[...] = matmul(proc_scatter[...], edge_slopes[...]).astype(jnp.bfloat16)
+    halo_back_copies = exchange(
+        "band",
+        lambda peer: back_ext.at[pl.ds(pl.multiple_of(rows + peer * halo_peer, halo_peer), halo_peer)],
+        lambda me: halo_back.at[block(me, halo_peer)],
+    )
+    halo_back[block(band, halo_peer), :] = back_ext[
+        pl.ds(pl.multiple_of(rows + band * halo_peer, halo_peer), halo_peer), :
+    ]
+    recv_whole[:, column(feat)] = back_ext[ext : ext + rows, :]
+    recv_copies = gather_held(recv_whole)
+    proc_summed = matmul(proc_scatter[ext : ext + rows, :], edge_values[...]).astype(jnp.bfloat16)
+    proc_whole[:, column(feat)] = proc_summed
+
+    tall = tall_part.shape[1] // bands
+    wide = wide_part.shape[1] // bands
+
+    def scatter_sum(part, land, place, size, value):
+        part[place] = value.astype(jnp.bfloat16)
+        return exchange(
+            "band",
+            lambda peer: part.at[place, block(peer, size)],
+            lambda me: land.at[place, me],
+        )
+
+    def add_up(copies, part, land, total, place, size):
+        arrive(copies)
+        mine = part[place, block(band, size), :]
+        land[place, band] = mine
+        value = land[place, 0].astype(jnp.float32)
+        for other in range(1, bands):
+            value = value + land[place, other].astype(jnp.float32)
+        total[place, block(band, size), :] = (value * scale).astype(jnp.bfloat16)
+        held = total.at[place, block(band, size)]
+        return exchange("band", lambda peer: held, lambda me: held)
+
+    grad_proc = scatter_sum(
+        wide_part, wide_land, 0, wide, inner_rows(proc_summed, cot_full[...])
+    )
+    edge_scatter(enc_scatter, g2m_src, 0, slots)
+    arrive(halo_back_copies)
+    back_send = (
+        back_ext[0:rows, :].astype(jnp.float32) + inner_rows(mesh_pick[...], halo_back[...])
+    ).astype(jnp.bfloat16)
+    send_whole[:, column(feat)] = back_send
+    send_copies = gather_held(send_whole)
+    proc_copies = gather_held(proc_whole)
+    copies = exchange(
+        "feat",
+        lambda peer: w_proc_out.at[:, column(peer)],
+        lambda me: proc_columns.at[block(me, width)],
+    )
+    proc_columns[block(feat, width), :] = w_proc_out[:, column(feat)]
+    proc_copies = proc_copies + copies
+    slice_copies = exchange(
+        "feat",
+        lambda peer: w_grid.at[block(peer, width)],
+        lambda me: grid_slice.at[:, column(me)],
+    )
+    grid_slice[:, column(feat)] = w_grid[block(feat, width), :]
+    grad_send = scatter_sum(tall_part, tall_land, 0, tall, inner_rows(mid_full[...], back_send))
+    grad_recv = scatter_sum(
+        tall_part, tall_land, 1, tall, inner_rows(mid_full[...], back_ext[ext : ext + rows, :])
+    )
+    arrive(send_weight_copies)
+    arrive(recv_weight_copies)
+    arrive(recv_copies)
+    back_sum = cot_full[...].astype(jnp.float32) + inner_columns(recv_whole[...], recv_full[...])
+    arrive(send_copies)
+    back_full[...] = (back_sum + inner_columns(send_whole[...], send_full[...])).astype(
+        jnp.bfloat16
+    )
+    back_enc = inner_columns(back_full[...], w_enc_out[...]).astype(jnp.bfloat16)
+    back_edge[...] = matmul(enc_gather[:, slots : slots + rows], back_enc)
+
+    def enc_backward(edges):
+        edge_slopes[edges, :] = (back_edge[edges, :] * enc_pre[edges, :]).astype(jnp.bfloat16)
+
+    per_chunk(enc_backward)
+    back_slot[...] = matmul(enc_scatter[...], edge_slopes[...]).astype(jnp.bfloat16)
+    slot_back_copies = exchange(
+        "band",
+        lambda peer: back_slot.at[block(peer, slot_peer)],
+        lambda me: slot_back.at[block(me, slot_peer)],
+    )
+    slot_back[block(band, slot_peer), :] = back_slot[block(band, slot_peer), :]
+    grad_mesh = scatter_sum(
+        tall_part,
+        tall_land,
+        2,
+        tall,
+        inner_rows(mesh_full[...], back_slot[slots : slots + rows, :]),
+    )
+    grad_enc = scatter_sum(
+        wide_part, wide_land, 1, wide, inner_rows(enc_whole[:, column(feat)], back_full[...])
+    )
+    proc_total = add_up(grad_proc, wide_part, wide_land, wide_sum, 0, wide)
+    arrive(slot_back_copies)
+    back_pgrid = inner_rows(grid_pick[...], slot_back[...]).astype(jnp.bfloat16)
+    pgrid_whole[:, column(feat)] = back_pgrid
+    grad_grid = scatter_sum(
+        tall_part, tall_land, 3, tall, inner_rows(grid_full[...], back_pgrid)
+    )
+    pgrid_copies = gather_held(pgrid_whole)
+    send_total = add_up(grad_send, tall_part, tall_land, tall_sum, 0, tall)
+    recv_total = add_up(grad_recv, tall_part, tall_land, tall_sum, 1, tall)
+    mesh_total = add_up(grad_mesh, tall_part, tall_land, tall_sum, 2, tall)
+    enc_total = add_up(grad_enc, wide_part, wide_land, wide_sum, 1, wide)
+    grid_total = add_up(grad_grid, tall_part, tall_land, tall_sum, 3, tall)
+    arrive(proc_copies)
+    mesh_out[...] = (
+        mid_full[:, column(feat)].astype(jnp.float32)
+        + matmul(proc_whole[...], proc_columns[...])
+    ).astype(jnp.bfloat16)
+    arrive(slice_copies)
+    arrive(pgrid_copies)
+    grid_grad[...] = inner_columns(pgrid_whole[...], grid_slice[...]).astype(jnp.bfloat16)
+    for total, held, place, target in (
+        (proc_total, wide_sum, 0, out_proc),
+        (send_total, tall_sum, 0, out_send),
+        (recv_total, tall_sum, 1, out_recv),
+        (mesh_total, tall_sum, 2, out_mesh),
+        (enc_total, wide_sum, 1, out_enc),
+        (grid_total, tall_sum, 3, out_grid),
+    ):
+        arrive(total)
+        target[...] = held[place].astype(target.dtype)
+    for copy in started:
+        copy.wait_send()
+
+
+def silu_slope_of(values):
+    sigma = sigmoid(values)
+    return sigma * (1.0 + values * (1.0 - sigma))
+
+
+def per_device(*arrays):
+    (grid_latent, mesh_latent, w_grid, _, w_enc_out) = arrays[:5]
+    grid_send, g2m_src, mesh_send = arrays[8], arrays[9], arrays[11]
+    bands = lax.axis_size("band")
+    feats = lax.axis_size("feat")
+    slot_peer, halo_peer = grid_send.shape[1], mesh_send.shape[1]
+    rows, width = mesh_latent.shape
+    grid_rows = grid_latent.shape[0]
+    latent = w_grid.shape[0]
+    edge_rows, lanes = g2m_src.shape
+    if slot_peer % 16 or halo_peer % 16 or width % (16 * bands) or 4 * edge_rows + 2 * bands > lanes:
+        return per_device_collectives(*arrays)
+    slots, halos = bands * slot_peer, bands * halo_peer
+    ext = rows + halos
+    edges = edge_rows * lanes
+    scale = 1.0 / math.sqrt(rows * bands)
+
+    def half(*shape):
+        return pltpu.VMEM(shape, jnp.bfloat16)
+
+    def full(*shape):
+        return pltpu.VMEM(shape, jnp.float32)
+
+    feat_phases, band_phases = 13, 16
+    scratch = [
+        pltpu.VMEM((lanes, lanes), jnp.int32),
+        pltpu.VMEM((lanes, lanes), jnp.int32),
+        half(grid_rows, latent),
+        half(rows, latent),
+        half(rows, latent),
+        half(latent, latent),
+        half(latent, latent),
+        half(latent, latent),
+        half(latent, width),
+        half(width, latent),
+        half(slots, grid_rows),
+        half(halos, rows),
+        half(edges, slots + rows),
+        half(slots + rows, edges),
+        half(edges, ext + rows),
+        half(ext + rows, edges),
+        half(slots + rows, width),
+        half(ext + rows, width),
+        half(slots, width),
+        half(halos, width),
+        full(edges, width),
+        full(edges, width),
+        half(edges, width),
+        half(edges, width),
+        half(rows, latent),
+        half(rows, latent),
+        half(rows, latent),
+        half(rows, latent),
+        half(rows, latent),
+        half(rows, latent),
+        half(ext + rows, width),
+        half(halos, width),
+        half(slots + rows, width),
+        half(slots, width),
+        half(grid_rows, latent),
+        half(4, latent, width),
+        half(4, bands, latent // bands, width),
+        half(4, latent, width),
+        half(2, width, latent),
+        half(2, bands, width // bands, latent),
+        half(2, width, latent),
+        pltpu.SemaphoreType.DMA((feat_phases, feats - 1)),
+        pltpu.SemaphoreType.DMA((feat_phases, feats - 1)),
+        pltpu.SemaphoreType.DMA((band_phases, bands - 1)),
+        pltpu.SemaphoreType.DMA((band_phases, bands - 1)),
+    ]
+    tall = jax.ShapeDtypeStruct((latent, width), jnp.float32)
+    wide = jax.ShapeDtypeStruct((width, latent), jnp.float32)
+    out_shape = (
+        jax.ShapeDtypeStruct((rows, width), jnp.bfloat16),
+        jax.ShapeDtypeStruct((grid_rows, width), jnp.bfloat16),
+        tall,
+        tall,
+        wide,
+        tall,
+        tall,
+        wide,
+    )
+    vmem = pl.BlockSpec(memory_space=pltpu.VMEM)
+    return pl.pallas_call(
+        functools.partial(fused_kernel, bands, feats, scale),
+        out_shape=out_shape,
+        in_specs=[vmem] * len(arrays),
+        out_specs=(vmem,) * len(out_shape),
+        scratch_shapes=scratch,
+        compiler_params=pltpu.CompilerParams(
+            collective_id=0, has_side_effects=True, vmem_limit_bytes=48 * 1024 * 1024
+        ),
+    )(*arrays)
+
+
 def solution(mesh):
     in_specs = (
         P("band", "feat"),

time: 259 us -> 96.8 us (0.37)
  waiting for transfers between devices: 83.1 us -> 0 us
  Pallas kernels: 0 us -> 78 us
  blocking collectives: 67 us -> 0 us
  starting transfers between devices: 35.9 us -> 0 us
  matrix products: 17.3 us -> 0 us
  between operations: 14.5 us -> 0.67 us
  local copies, waits for them, and re-layouts: 28.9 us -> 17.5 us
  other arithmetic: 10.6 us -> 0 us
    pallas_call x0 -> x1, Pallas kernels: none -> 78 us  [per_device(): pl.pallas_call(functools.partial(fused_kernel, bands, feats, scale), out_...]
    psum x1 -> x0, waiting for transfers between devices: 60.1 us -> none  [per_device(): lax.psum((grad_grid_w, grad_mesh_w, grad_enc_out, grad_send, grad_recv, g...]
    all_gather x10 -> x0, blocking collectives: 59.9 us -> none  [the longest x1 6.78 us: per_device(): mesh_full = lax.all_gather(mesh_latent, 'feat', axis=1, tiled=True)]
    all_to_all x8 -> x0, starting transfers between devices: 35.8 us -> none  [the longest x1 6.36 us: per_device(): lax.all_to_all(outgoing, 'band', split_axis=0, concat_axis=0, tiled=True)]
    all_to_all x8 -> x0, waiting for transfers between devices: 23 us -> none  [the longest x1 6.51 us: per_device(): lax.all_to_all(back_slot.reshape(bands, slot_rows // bands, hidden_dev),...]
    gather x8 -> x0, local copies, waits for them, and re-layouts: 21.4 us -> none  [the longest x1 3.21 us: per_device(): jnp.take(back_proc, proc_target, axis=0).astype(jnp.float32)]
    dot_general x22 -> x0, matrix products: 17.3 us -> none  [the longest x11 11 us: inner_rows(): lax.dot_general(left, right, (((0,), (0,)), ((), ())), preferred_element_...]
    unnamed x40 -> x38, local copies, waits for them, and re-layouts: 6.55 us -> 17.5 us
  transfers between devices with their start and end apart: 9 -> 0, of which waited for: 7 -> 0; matrix products, arithmetic and copies ran while one was open for 8% -> 0% of each run, Pallas kernels for 0% -> 0%
where the time goes in v1:
time: 96.8 us; the launch traced here: 96.2 us
  Pallas kernels  78 us (81%)
  local copies, waits for them, and re-layouts  17.5 us (18%)
    pallas_call x1, Pallas kernels, per_device(): pl.pallas_call(functools.partial(fused_kernel, bands, feats, scale), out_...  78 us
    unnamed x38, local copies, waits for them, and re-layouts  17.5 us

profile of v1, /device:TPU:0, one launch (start us, length us, event | category | flops | bytes accessed | tf_op | source)
XLA Modules:
  0.0 96.2 jit_solution(11380115714753042556)
XLA Ops:
  0.6 0.0 copy-start
  0.6 0.9 copy-done
  1.5 0.0 copy-start.1
  1.5 0.9 copy-done.1
  2.4 0.0 copy-start.2
  2.5 0.9 copy-done.2
  3.4 0.0 copy-start.3
  3.4 0.9 copy-done.3
  4.3 0.0 copy-start.4
  4.3 0.9 copy-done.4
  5.2 0.0 copy-start.5
  5.2 0.9 copy-done.5
  6.1 0.0 copy-start.6
  6.1 0.8 copy-done.6
  6.9 0.0 copy-start.7
  6.9 0.8 copy-done.7
  7.8 0.8 copy-done.8
  8.6 0.7 copy-done.9
  9.3 0.7 copy-done.10
  10.0 0.7 copy-done.11
  10.7 0.7 copy-done.12
  11.3 0.7 copy-done.13
  12.0 0.7 copy-done.14
  12.7 78.0 %shard_map.206 = (bf16[256,128]{1,0:T(8,128)(2,1)S(1)}, bf16[256,128]{1,0:T(8,128)(2,1)S(1)}, f32[512,128]{1,0:T(8,128)S(1)}, f32[512,128]{1,0:T(8,128)S(1)}, f3...) custom-call(bf16[256,128]{1,0:T(8,128)(2,1)S(1)} %copy-done.6, ...), custom_call_target="tpu_custom_call" | custom-call | tf_op jit(solution)/shard_map/pallas_call | solution.py:661
  90.7 0.6 copy.31
  91.4 0.6 copy.32
  92.0 0.7 copy.33
  92.7 0.7 copy.34
  93.4 0.7 copy.35
  94.1 0.7 copy.36
  94.8 0.7 copy.37
  95.5 0.7 copy.38
  (7 shorter events, 0.0 us)
Async XLA Ops:
  0.6 0.9 copy-start
  1.5 0.9 copy-start.1
  2.4 0.9 copy-start.2
  3.4 0.9 copy-start.3
  4.3 0.9 copy-start.4
  5.2 0.9 copy-start.5
  6.1 0.8 copy-start.6
  6.9 0.8 copy-start.7
  7.7 0.8 copy-start.8
  8.6 0.7 copy-start.9
  9.3 0.7 copy-start.10
  10.0 0.7 copy-start.11
  10.7 0.7 copy-start.12
  11.3 0.7 copy-start.13
  12.0 0.7 copy-start.14

commit v2 on v1

--- a/solution.py
+++ b/solution.py
@@ -181,27 +181,28 @@
     scale,
     grid_latent,
     mesh_latent,
-    w_grid,
-    w_mesh,
-    w_enc_out,
-    w_send,
-    w_recv,
-    w_proc_out,
-    grid_send,
+    w_grid_hbm,
+    w_mesh_hbm,
+    w_enc_hbm,
+    w_send_hbm,
+    w_recv_hbm,
+    w_proc_hbm,
+    grid_send_hbm,
     g2m_src,
     g2m_dst,
-    mesh_send,
+    mesh_send_hbm,
     m2m_src,
     m2m_dst,
     cotangent,
     mesh_out,
     grid_grad,
-    out_grid,
-    out_mesh,
-    out_enc,
-    out_send,
-    out_recv,
-    out_proc,
+    tall_out,
+    wide_out,
+    w_grid,
+    w_mesh,
+    w_proc_out,
+    grid_send,
+    mesh_send,
     index_rows,
     index_columns,
     grid_full,
@@ -247,6 +248,7 @@
     feat_recv_sem,
     band_send_sem,
     band_recv_sem,
+    stage_sem,
 ):
     band = lax.axis_index("band")
     feat = lax.axis_index("feat")
@@ -267,6 +269,30 @@
 
     def block(place, size):
         return pl.ds(pl.multiple_of(place * size, size), size)
+
+    staged = []
+
+    def stage(source, target):
+        copy = pltpu.make_async_copy(source, target, stage_sem.at[len(staged)])
+        copy.start()
+        staged.append(copy)
+        return copy
+
+    index_rows[...] = jnp.zeros_like(index_rows)
+    index_copies = [
+        stage(source, index_rows.at[pl.ds(place * edge_rows, edge_rows)])
+        for place, source in enumerate((g2m_src, g2m_dst, m2m_src, m2m_dst))
+    ]
+    index_copies += [stage(grid_send_hbm, grid_send), stage(mesh_send_hbm, mesh_send)]
+    w_grid_copy = stage(w_grid_hbm, w_grid)
+    grid_own = stage(grid_latent, grid_full.at[:, column(feat)])
+    mesh_own = stage(mesh_latent, mesh_full.at[:, column(feat)])
+    w_mesh_copy = stage(w_mesh_hbm, w_mesh)
+    enc_own = stage(w_enc_hbm, enc_full.at[block(feat, width)])
+    cot_own = stage(cotangent, cot_full.at[:, column(feat)])
+    w_proc_copy = stage(w_proc_hbm, w_proc_out)
+    send_own = stage(w_send_hbm, send_full.at[:, column(feat)])
+    recv_own = stage(w_recv_hbm, recv_full.at[:, column(feat)])
 
     barrier = pltpu.get_barrier_semaphore()
     for step in range(1, bands):
@@ -316,9 +342,7 @@
             copy.wait_recv()
 
     def gather_columns(source, target):
-        copies = exchange("feat", lambda peer: source, lambda me: target.at[:, column(me)])
-        target[:, column(feat)] = source[...]
-        return copies
+        return exchange("feat", lambda peer: source, lambda me: target.at[:, column(me)])
 
     def gather_held(target):
         mine = target.at[:, column(feat)]
@@ -327,11 +351,8 @@
     grid_copies = gather_columns(grid_latent, grid_full)
     mesh_copies = gather_columns(mesh_latent, mesh_full)
 
-    index_rows[...] = jnp.zeros_like(index_rows)
-    index_rows[0:edge_rows, :] = g2m_src[...]
-    index_rows[edge_rows : 2 * edge_rows, :] = g2m_dst[...]
-    index_rows[2 * edge_rows : 3 * edge_rows, :] = m2m_src[...]
-    index_rows[3 * edge_rows : 4 * edge_rows, :] = m2m_dst[...]
+    for copy in index_copies:
+        copy.wait()
     index_rows[4 * edge_rows : 4 * edge_rows + bands, 0:slot_peer] = grid_send[...]
     index_rows[4 * edge_rows + bands : 4 * edge_rows + 2 * bands, 0:halo_peer] = mesh_send[...]
     index_columns[...] = index_rows[...].T
@@ -351,11 +372,13 @@
     def edge_scatter(target, index, start, count):
         place = lax.broadcasted_iota(jnp.int32, (count, lanes), 0)
         for row in range(edge_rows):
-            chosen = index[row : row + 1, :]
+            chosen = index_rows[index + row : index + row + 1, :]
             target[start : start + count, row * lanes : (row + 1) * lanes] = hot(chosen == place)
 
     picks(grid_pick, 4 * edge_rows, slot_peer, grid_rows)
 
+    grid_own.wait()
+    w_grid_copy.wait()
     arrive(grid_copies)
     proj_grid = matmul(grid_full[...], w_grid[...]).astype(jnp.bfloat16)
     outgoing[...] = matmul(grid_pick[...], proj_grid).astype(jnp.bfloat16)
@@ -365,16 +388,17 @@
         lambda me: enc_rows.at[block(me, slot_peer)],
     )
     enc_rows[block(band, slot_peer), :] = outgoing[block(band, slot_peer), :]
+    mesh_own.wait()
+    w_mesh_copy.wait()
     arrive(mesh_copies)
-    enc_full[block(feat, width), :] = w_enc_out[...]
     enc_weight_copies = exchange(
-        "feat", lambda peer: w_enc_out, lambda me: enc_full.at[block(me, width)]
+        "feat", lambda peer: w_enc_hbm, lambda me: enc_full.at[block(me, width)]
     )
     cot_copies = gather_columns(cotangent, cot_full)
     enc_rows[slots : slots + rows, :] = matmul(mesh_full[...], w_mesh[...]).astype(jnp.bfloat16)
     edge_gather(enc_gather, 0, 0, slots)
     edge_gather(enc_gather, edge_rows, slots, rows)
-    edge_scatter(enc_scatter, g2m_dst, slots, rows)
+    edge_scatter(enc_scatter, edge_rows, slots, rows)
 
     def per_chunk(body):
         size = 2 * lanes
@@ -404,30 +428,35 @@
     picks(mesh_pick, 4 * edge_rows + bands, halo_peer, rows)
     edge_gather(proc_gather, 2 * edge_rows, 0, ext)
     edge_gather(proc_gather, 3 * edge_rows, ext, rows)
+    enc_own.wait()
     arrive(enc_weight_copies)
     arrive(enc_copies)
+    send_own.wait()
     mid_full[...] = (
         mesh_full[...].astype(jnp.float32) + matmul(enc_whole[...], enc_full[...])
     ).astype(jnp.bfloat16)
-    proj_send = matmul(mid_full[...], w_send[...]).astype(jnp.bfloat16)
+    proj_send = matmul(mid_full[...], send_full[:, column(feat)]).astype(jnp.bfloat16)
     halo_out[...] = matmul(mesh_pick[...], proj_send).astype(jnp.bfloat16)
     halo_copies = exchange(
         "band",
         lambda peer: halo_out.at[block(peer, halo_peer)],
         lambda me: proc_rows.at[pl.ds(pl.multiple_of(rows + me * halo_peer, halo_peer), halo_peer)],
     )
-    send_weight_copies = gather_columns(w_send, send_full)
-    recv_weight_copies = gather_columns(w_recv, recv_full)
+    send_weight_copies = gather_columns(w_send_hbm, send_full)
+    recv_weight_copies = gather_columns(w_recv_hbm, recv_full)
+    recv_own.wait()
     proc_rows[pl.ds(pl.multiple_of(rows + band * halo_peer, halo_peer), halo_peer), :] = halo_out[
         block(band, halo_peer), :
     ]
     proc_rows[0:rows, :] = proj_send
-    proc_rows[ext : ext + rows, :] = matmul(mid_full[...], w_recv[...]).astype(jnp.bfloat16)
+    proc_rows[ext : ext + rows, :] = matmul(mid_full[...], recv_full[:, column(feat)]).astype(jnp.bfloat16)
+    cot_own.wait()
+    w_proc_copy.wait()
     arrive(cot_copies)
     back_proc = inner_columns(cot_full[...], w_proc_out[...]).astype(jnp.bfloat16)
     back_edge[...] = matmul(proc_gather[:, ext : ext + rows], back_proc)
-    edge_scatter(proc_scatter, m2m_src, 0, ext)
-    edge_scatter(proc_scatter, m2m_dst, ext, rows)
+    edge_scatter(proc_scatter, 2 * edge_rows, 0, ext)
+    edge_scatter(proc_scatter, 3 * edge_rows, ext, rows)
     arrive(halo_copies)
 
     def proc_forward(edges):
@@ -477,7 +506,7 @@
     grad_proc = scatter_sum(
         wide_part, wide_land, 0, wide, inner_rows(proc_summed, cot_full[...])
     )
-    edge_scatter(enc_scatter, g2m_src, 0, slots)
+    edge_scatter(enc_scatter, 0, 0, slots)
     arrive(halo_back_copies)
     back_send = (
         back_ext[0:rows, :].astype(jnp.float32) + inner_rows(mesh_pick[...], halo_back[...])
@@ -510,7 +539,7 @@
     back_full[...] = (back_sum + inner_columns(send_whole[...], send_full[...])).astype(
         jnp.bfloat16
     )
-    back_enc = inner_columns(back_full[...], w_enc_out[...]).astype(jnp.bfloat16)
+    back_enc = inner_columns(back_full[...], enc_full[block(feat, width), :]).astype(jnp.bfloat16)
     back_edge[...] = matmul(enc_gather[:, slots : slots + rows], back_enc)
 
     def enc_backward(edges):
@@ -555,18 +584,62 @@
     arrive(slice_copies)
     arrive(pgrid_copies)
     grid_grad[...] = inner_columns(pgrid_whole[...], grid_slice[...]).astype(jnp.bfloat16)
-    for total, held, place, target in (
-        (proc_total, wide_sum, 0, out_proc),
-        (send_total, tall_sum, 0, out_send),
-        (recv_total, tall_sum, 1, out_recv),
-        (mesh_total, tall_sum, 2, out_mesh),
-        (enc_total, wide_sum, 1, out_enc),
-        (grid_total, tall_sum, 3, out_grid),
-    ):
+    for total in (proc_total, send_total, recv_total, mesh_total, enc_total, grid_total):
         arrive(total)
-        target[...] = held[place].astype(target.dtype)
+    tall_out[...] = tall_sum[...]
+    wide_out[...] = wide_sum[...]
     for copy in started:
         copy.wait_send()
+
+
+def write_kernel(
+    mesh_held,
+    grid_held,
+    tall_hbm,
+    wide_hbm,
+    mesh_out,
+    grid_grad,
+    out_grid,
+    out_mesh,
+    out_enc,
+    out_send,
+    out_recv,
+    out_proc,
+    tall_held,
+    wide_held,
+    tall_wide,
+    wide_wide,
+    copy_sem,
+    load_sem,
+):
+    loads = [
+        pltpu.make_async_copy(tall_hbm, tall_held, load_sem.at[0]),
+        pltpu.make_async_copy(wide_hbm, wide_held, load_sem.at[1]),
+    ]
+    for load in loads:
+        load.start()
+    copies = [
+        pltpu.make_async_copy(mesh_held, mesh_out, copy_sem.at[0]),
+        pltpu.make_async_copy(grid_held, grid_grad, copy_sem.at[1]),
+    ]
+    for copy in copies:
+        copy.start()
+    for load in loads:
+        load.wait()
+    for held, wide, place, target in (
+        (tall_held, tall_wide, 0, out_send),
+        (tall_held, tall_wide, 1, out_recv),
+        (tall_held, tall_wide, 2, out_mesh),
+        (tall_held, tall_wide, 3, out_grid),
+        (wide_held, wide_wide, 0, out_proc),
+        (wide_held, wide_wide, 1, out_enc),
+    ):
+        wide[place] = held[place].astype(jnp.float32)
+        copy = pltpu.make_async_copy(wide.at[place], target, copy_sem.at[len(copies)])
+        copy.start()
+        copies.append(copy)
+    for copy in copies:
+        copy.wait()
 
 
 def silu_slope_of(values):
@@ -584,7 +657,7 @@
     grid_rows = grid_latent.shape[0]
     latent = w_grid.shape[0]
     edge_rows, lanes = g2m_src.shape
-    if slot_peer % 16 or halo_peer % 16 or width % (16 * bands) or 4 * edge_rows + 2 * bands > lanes:
+    if edge_rows % 8 or slot_peer % 16 or halo_peer % 16 or width % (16 * bands) or 4 * edge_rows + 2 * bands > lanes:
         return per_device_collectives(*arrays)
     slots, halos = bands * slot_peer, bands * halo_peer
     ext = rows + halos
@@ -599,6 +672,11 @@
 
     feat_phases, band_phases = 13, 16
     scratch = [
+        half(latent, width),
+        half(latent, width),
+        half(width, latent),
+        pltpu.VMEM(grid_send.shape, jnp.int32),
+        pltpu.VMEM(mesh_send.shape, jnp.int32),
         pltpu.VMEM((lanes, lanes), jnp.int32),
         pltpu.VMEM((lanes, lanes), jnp.int32),
         half(grid_rows, latent),
@@ -644,30 +722,45 @@
         pltpu.SemaphoreType.DMA((feat_phases, feats - 1)),
         pltpu.SemaphoreType.DMA((band_phases, bands - 1)),
         pltpu.SemaphoreType.DMA((band_phases, bands - 1)),
+        pltpu.SemaphoreType.DMA((len(arrays),)),
     ]
     tall = jax.ShapeDtypeStruct((latent, width), jnp.float32)
     wide = jax.ShapeDtypeStruct((width, latent), jnp.float32)
-    out_shape = (
+    nodes = (
         jax.ShapeDtypeStruct((rows, width), jnp.bfloat16),
         jax.ShapeDtypeStruct((grid_rows, width), jnp.bfloat16),
-        tall,
-        tall,
-        wide,
-        tall,
-        tall,
-        wide,
+    )
+    sums = (
+        jax.ShapeDtypeStruct((4, latent, width), jnp.bfloat16),
+        jax.ShapeDtypeStruct((2, width, latent), jnp.bfloat16),
     )
     vmem = pl.BlockSpec(memory_space=pltpu.VMEM)
-    return pl.pallas_call(
+    hbm = pl.BlockSpec(memory_space=pltpu.HBM)
+    held = pl.pallas_call(
         functools.partial(fused_kernel, bands, feats, scale),
-        out_shape=out_shape,
-        in_specs=[vmem] * len(arrays),
-        out_specs=(vmem,) * len(out_shape),
+        out_shape=nodes + sums,
+        in_specs=[hbm] * len(arrays),
+        out_specs=(vmem,) * 4,
         scratch_shapes=scratch,
         compiler_params=pltpu.CompilerParams(
-            collective_id=0, has_side_effects=True, vmem_limit_bytes=48 * 1024 * 1024
+            collective_id=0, has_side_effects=True, vmem_limit_bytes=61 * 1024 * 1024
         ),
     )(*arrays)
+    return pl.pallas_call(
+        write_kernel,
+        out_shape=nodes + (tall, tall, wide, tall, tall, wide),
+        in_specs=[hbm] * 4,
+        out_specs=(hbm,) * 8,
+        scratch_shapes=[
+            half(4, latent, width),
+            half(2, width, latent),
+            full(4, latent, width),
+            full(2, width, latent),
+            pltpu.SemaphoreType.DMA((8,)),
+            pltpu.SemaphoreType.DMA((2,)),
+        ],
+        compiler_params=pltpu.CompilerParams(vmem_limit_bytes=61 * 1024 * 1024),
+    )(*held)
 
 
 def solution(mesh):

time: 96.8 us -> 85.9 us (0.89)
  local copies, waits for them, and re-layouts: 17.5 us -> 0 us
  Pallas kernels: 78 us -> 85 us
    unnamed x38 -> x0, local copies, waits for them, and re-layouts: 17.5 us -> none
    pallas_call x0 -> x1, Pallas kernels: none -> 5.17 us  [per_device(): pl.pallas_call(write_kernel, out_shape=nodes + (tall, tall, wide, tall, t...]
    pallas_call x1, Pallas kernels: 78 us -> 79.8 us  [per_device(): pl.pallas_call(functools.partial(fused_kernel, bands, feats, scale), out_...]
where the time goes in v2:
time: 85.9 us; the launch traced here: 85.6 us
  Pallas kernels  85 us (99%)
    pallas_call x1, Pallas kernels, per_device(): pl.pallas_call(functools.partial(fused_kernel, bands, feats, scale), out_...  79.8 us
    pallas_call x1, Pallas kernels, per_device(): pl.pallas_call(write_kernel, out_shape=nodes + (tall, tall, wide, tall, t...  5.17 us

profile of v2, /device:TPU:0, one launch (start us, length us, event | category | flops | bytes accessed | tf_op | source)
XLA Modules:
  0.0 85.6 jit_solution(2265955239663197951)
XLA Ops:
  0.6 79.8 %shard_map.206 = (bf16[256,128]{1,0:T(8,128)(2,1)}, bf16[256,128]{1,0:T(8,128)(2,1)}, bf16[4,512,128]{2,1,0:T(8,128)(2,1)}, bf16[2,128,512]{2,1,0:T(8,128)(2,1)}) custom-call(bf16[256,128]{1,0:T(8,128)(2,1)} %grid_latent.1, bf16[256,128]{1,0:T(8,128)(2,1)} %mesh_latent.1, bf16[512,128]{1,0:T(8,128)(2,1)} %w_grid_hbm.1, bf16[512,128]{1,0:T(8,128)(2,1)} %w_mesh_hbm.1, ...), custom_call_target="tpu_custom_call" | custom-call | tf_op jit(solution)/shard_map/pallas_call | solution.py:739
  80.5 5.2 %shard_map.207 = (bf16[256,128]{1,0:T(8,128)(2,1)}, bf16[256,128]{1,0:T(8,128)(2,1)}, f32[512,128]{1,0:T(8,128)}, f32[512,128]{1,0:T(8,128)}, f32[128,512]{1,0:T...) custom-call(bf16[256,128]{1,0:T(8,128)(2,1)} %get-tuple-element.12.mesh_held, ...), custom_call_target="tpu_custom_call" | custom-call | tf_op jit(solution)/shard_map/pallas_call | solution.py:749

commit v3 on v2

--- a/solution.py
+++ b/solution.py
@@ -337,16 +337,52 @@
         started.extend(copies)
         return copies
 
+    near = feat + 1 - 2 * lax.rem(feat, 2)
+    far = lax.rem(feat + 2, feats)
+
+    def spread(source, place):
+        phase = counts["feat"]
+        counts["feat"] += 1
+
+        def send(step, part, target, peer):
+            copy = pltpu.make_async_remote_copy(
+                src_ref=part,
+                dst_ref=target,
+                send_sem=feat_send_sem.at[phase, step],
+                recv_sem=feat_recv_sem.at[phase, step],
+                device_id={"feat": peer},
+                device_id_type=pl.DeviceIdType.MESH,
+            )
+            started.append(copy)
+            return copy
+
+        across = send(0, source, place(feat), far)
+        across.start()
+        beside = send(1, source, place(feat), near)
+        beside.start()
+        onward = send(2, place(far), place(far), near)
+        return {"across": across, "beside": beside, "onward": onward, "relayed": False}
+
+    def relay(copies):
+        if not copies["relayed"]:
+            copies["across"].wait_recv()
+            copies["onward"].start()
+            copies["relayed"] = True
+
     def arrive(copies):
-        for copy in copies:
-            copy.wait_recv()
+        if isinstance(copies, dict):
+            relay(copies)
+            copies["beside"].wait_recv()
+            copies["onward"].wait_recv()
+        else:
+            for copy in copies:
+                copy.wait_recv()
 
     def gather_columns(source, target):
-        return exchange("feat", lambda peer: source, lambda me: target.at[:, column(me)])
+        return spread(source, lambda owner: target.at[:, column(owner)])
 
     def gather_held(target):
-        mine = target.at[:, column(feat)]
-        return exchange("feat", lambda peer: mine, lambda me: mine)
+        return spread(target.at[:, column(feat)], lambda owner: target.at[:, column(owner)])
 
     grid_copies = gather_columns(grid_latent, grid_full)
     mesh_copies = gather_columns(mesh_latent, mesh_full)
@@ -391,9 +427,7 @@
     mesh_own.wait()
     w_mesh_copy.wait()
     arrive(mesh_copies)
-    enc_weight_copies = exchange(
-        "feat", lambda peer: w_enc_hbm, lambda me: enc_full.at[block(me, width)]
-    )
+    enc_weight_copies = spread(w_enc_hbm, lambda owner: enc_full.at[block(owner, width)])
     cot_copies = gather_columns(cotangent, cot_full)
     enc_rows[slots : slots + rows, :] = matmul(mesh_full[...], w_mesh[...]).astype(jnp.bfloat16)
     edge_gather(enc_gather, 0, 0, slots)
@@ -420,6 +454,8 @@
     enc_summed = matmul(enc_scatter[slots : slots + rows, :], edge_values[...])
     enc_whole[:, column(feat)] = enc_summed.astype(jnp.bfloat16)
     enc_copies = gather_held(enc_whole)
+    relay(enc_weight_copies)
+    relay(cot_copies)
 
     def enc_slope(edges):
         enc_pre[edges, :] = silu_slope_of(enc_pre[edges, :])
@@ -478,6 +514,8 @@
     ]
     recv_whole[:, column(feat)] = back_ext[ext : ext + rows, :]
     recv_copies = gather_held(recv_whole)
+    relay(send_weight_copies)
+    relay(recv_weight_copies)
     proc_summed = matmul(proc_scatter[ext : ext + rows, :], edge_values[...]).astype(jnp.bfloat16)
     proc_whole[:, column(feat)] = proc_summed
 
@@ -507,6 +545,7 @@
         wide_part, wide_land, 0, wide, inner_rows(proc_summed, cot_full[...])
     )
     edge_scatter(enc_scatter, 0, 0, slots)
+    relay(recv_copies)
     arrive(halo_back_copies)
     back_send = (
         back_ext[0:rows, :].astype(jnp.float32) + inner_rows(mesh_pick[...], halo_back[...])
@@ -514,13 +553,12 @@
     send_whole[:, column(feat)] = back_send
     send_copies = gather_held(send_whole)
     proc_copies = gather_held(proc_whole)
-    copies = exchange(
+    column_copies = exchange(
         "feat",
         lambda peer: w_proc_out.at[:, column(peer)],
         lambda me: proc_columns.at[block(me, width)],
     )
     proc_columns[block(feat, width), :] = w_proc_out[:, column(feat)]
-    proc_copies = proc_copies + copies
     slice_copies = exchange(
         "feat",
         lambda peer: w_grid.at[block(peer, width)],
@@ -535,6 +573,8 @@
     arrive(recv_weight_copies)
     arrive(recv_copies)
     back_sum = cot_full[...].astype(jnp.float32) + inner_columns(recv_whole[...], recv_full[...])
+    relay(send_copies)
+    proc_total = add_up(grad_proc, wide_part, wide_land, wide_sum, 0, wide)
     arrive(send_copies)
     back_full[...] = (back_sum + inner_columns(send_whole[...], send_full[...])).astype(
         jnp.bfloat16
@@ -563,7 +603,8 @@
     grad_enc = scatter_sum(
         wide_part, wide_land, 1, wide, inner_rows(enc_whole[:, column(feat)], back_full[...])
     )
-    proc_total = add_up(grad_proc, wide_part, wide_land, wide_sum, 0, wide)
+    send_total = add_up(grad_send, tall_part, tall_land, tall_sum, 0, tall)
+    recv_total = add_up(grad_recv, tall_part, tall_land, tall_sum, 1, tall)
     arrive(slot_back_copies)
     back_pgrid = inner_rows(grid_pick[...], slot_back[...]).astype(jnp.bfloat16)
     pgrid_whole[:, column(feat)] = back_pgrid
@@ -571,12 +612,11 @@
         tall_part, tall_land, 3, tall, inner_rows(grid_full[...], back_pgrid)
     )
     pgrid_copies = gather_held(pgrid_whole)
-    send_total = add_up(grad_send, tall_part, tall_land, tall_sum, 0, tall)
-    recv_total = add_up(grad_recv, tall_part, tall_land, tall_sum, 1, tall)
     mesh_total = add_up(grad_mesh, tall_part, tall_land, tall_sum, 2, tall)
     enc_total = add_up(grad_enc, wide_part, wide_land, wide_sum, 1, wide)
     grid_total = add_up(grad_grid, tall_part, tall_land, tall_sum, 3, tall)
     arrive(proc_copies)
+    arrive(column_copies)
     mesh_out[...] = (
         mid_full[:, column(feat)].astype(jnp.float32)
         + matmul(proc_whole[...], proc_columns[...])
@@ -657,7 +697,7 @@
     grid_rows = grid_latent.shape[0]
     latent = w_grid.shape[0]
     edge_rows, lanes = g2m_src.shape
-    if edge_rows % 8 or slot_peer % 16 or halo_peer % 16 or width % (16 * bands) or 4 * edge_rows + 2 * bands > lanes:
+    if feats != 4 or edge_rows % 8 or slot_peer % 16 or halo_peer % 16 or width % (16 * bands) or 4 * edge_rows + 2 * bands > lanes:
         return per_device_collectives(*arrays)
     slots, halos = bands * slot_peer, bands * halo_peer
     ext = rows + halos

time: 85.9 us -> 79.1 us (0.921)
  Pallas kernels: 85 us -> 78.3 us
    pallas_call x1, Pallas kernels: 79.8 us -> 73.1 us  [per_device(): pl.pallas_call(functools.partial(fused_kernel, bands, feats, scale), out_...]
where the time goes in v3:
time: 79.1 us; the launch traced here: 78.9 us
  Pallas kernels  78.3 us (99%)
    pallas_call x1, Pallas kernels, per_device(): pl.pallas_call(functools.partial(fused_kernel, bands, feats, scale), out_...  73.1 us
    pallas_call x1, Pallas kernels, per_device(): pl.pallas_call(write_kernel, out_shape=nodes + (tall, tall, wide, tall, t...  5.17 us

profile of v3, /device:TPU:0, one launch (start us, length us, event | category | flops | bytes accessed | tf_op | source)
XLA Modules:
  0.0 78.9 jit_solution(9157787606405938156)
XLA Ops:
  0.6 73.1 %shard_map.206 = (bf16[256,128]{1,0:T(8,128)(2,1)}, bf16[256,128]{1,0:T(8,128)(2,1)}, bf16[4,512,128]{2,1,0:T(8,128)(2,1)}, bf16[2,128,512]{2,1,0:T(8,128)(2,1)}) custom-call(bf16[256,128]{1,0:T(8,128)(2,1)} %grid_latent.1, bf16[256,128]{1,0:T(8,128)(2,1)} %mesh_latent.1, bf16[512,128]{1,0:T(8,128)(2,1)} %w_grid_hbm.1, bf16[512,128]{1,0:T(8,128)(2,1)} %w_mesh_hbm.1, ...), custom_call_target="tpu_custom_call" | custom-call | tf_op jit(solution)/shard_map/pallas_call | solution.py:779
  73.7 5.2 %shard_map.207 = (bf16[256,128]{1,0:T(8,128)(2,1)}, bf16[256,128]{1,0:T(8,128)(2,1)}, f32[512,128]{1,0:T(8,128)}, f32[512,128]{1,0:T(8,128)}, f32[128,512]{1,0:T...) custom-call(bf16[256,128]{1,0:T(8,128)(2,1)} %get-tuple-element.12.mesh_held, ...), custom_call_target="tpu_custom_call" | custom-call | tf_op jit(solution)/shard_map/pallas_call | solution.py:789
